TPU v7x, 256 devices: a whole 4x4x8 slice. The times are simulated.
256 devices in a mesh: blk: 32 (over x_lo, z, core), uly: 8 (over y, x_hi).
Axes of the slice: x: 4 (x_hi: 2, x_lo: 2; x = x_hi * 2 + x_lo), y: 4, z: 8, core: 2. Of those that a mesh axis runs over, the one named last changes fastest.
Arguments:
- joint_qkv: bfloat16 [16384, 3, 3072], P(('blk', 'uly')), may hold values from -40 to 40
- text_count: int32 [1], replicated, may hold values from 1 to 512
- region_ids: int32 [16384], P('blk'), may hold values from 0 to 4
- region_identity: int32 [4], replicated, may hold values from 0 to 3, each once
- id_feats: bfloat16 [4, 256, 3072], P(None, 'blk'), may hold values from -6 to 6
- resample_mix: bfloat16 [32, 256], P(None, 'blk'), may hold values from -0.375 to 0.375
- latents: bfloat16 [32, 3072], replicated, may hold values from -6 to 6
- id_gain: float32 [3072], replicated, may hold values from 0.25 to 1.75
- id_kv_weight: bfloat16 [3072, 2, 3072], P(None, None, 'uly'), may hold values from -0.109375 to 0.109375
- out_weight: bfloat16 [3072, 3072], P('uly'), may hold values from -0.109375 to 0.109375
Outputs:
- output: bfloat16 [16384, 3072], P(('blk', 'uly'))
Inputs may be any that keep to these rules, and one draw needn't show every extreme that they name: `region_identity`: A permutation of 0 to 3.
All inputs are finite; a program needn't handle non-finite values.
Results may differ from a plain program's by a relative error of at most 0.0095.
Values may be sent and summed in bfloat16 or wider, within the bound.
No kernel may reach another device: no remote copies, remote signals or barrier semaphores. Data moves between devices by JAX's collectives and lax.ppermute only.
A program may use at most 128 MiB of HBM per device.

v0:
```python
import math

import jax
import jax.numpy as jnp
from jax import lax
from jax.sharding import PartitionSpec as P

HEAD = 128
TXT = 512
SUBJ = 4
IDTOK = 32


def normalize(summed, id_gain):
    mean_square = jnp.mean(summed * summed, axis=-1, keepdims=True)
    return (summed * lax.rsqrt(mean_square + 1e-06) * id_gain).astype(jnp.bfloat16)


def on_device(
    joint_qkv,
    text_count,
    region_ids,
    region_identity,
    id_feats,
    resample_mix,
    latents,
    id_gain,
    id_kv_weight,
    out_weight,
):
    uly_count = lax.axis_size("uly")
    tok_dev = joint_qkv.shape[0]
    tok_blk = tok_dev * uly_count
    width = joint_qkv.shape[2]
    width_here = id_kv_weight.shape[2]
    heads_here = width_here // HEAD
    score_scale = 1.0 / math.sqrt(HEAD)
    block_start = lax.axis_index("blk") * tok_blk
    split = lax.all_to_all(joint_qkv, "uly", split_axis=2, concat_axis=0, tiled=True)
    queries = split[:, 0].reshape(tok_blk, heads_here, HEAD)
    key_vals = split[:, 1:3]

    def absorb_one(carried, shard_keys, offset):
        peak_old, totals_old, accum_old = carried
        keys_block = shard_keys[:, 0].reshape(tok_blk, heads_here, HEAD)
        values_block = shard_keys[:, 1].reshape(tok_blk, heads_here, HEAD)
        positions = offset + jnp.arange(tok_blk, dtype=jnp.int32)
        usable = (positions >= TXT) | (positions < text_count[0])
        scores = (
            jnp.einsum("qhe,khe->qhk", queries, keys_block, preferred_element_type=jnp.float32)
            * score_scale
        )
        scores = jnp.where(usable[None, None, :], scores, -1e30)
        peak_new = jnp.maximum(peak_old, jnp.max(scores, axis=-1))
        factor = jnp.exp(peak_old - peak_new)
        exponent = jnp.exp(scores - peak_new[:, :, None])
        totals_new = totals_old * factor + jnp.sum(exponent, axis=-1)
        product = jnp.einsum(
            "qhk,khe->qhe",
            exponent.astype(jnp.bfloat16),
            values_block,
            preferred_element_type=jnp.float32,
        )
        accum_new = accum_old * factor[:, :, None] + product
        return (peak_new, totals_new, accum_new)

    start_state = (
        jnp.full((tok_blk, heads_here), -1e30, jnp.float32),
        jnp.zeros((tok_blk, heads_here), jnp.float32),
        jnp.zeros((tok_blk, heads_here, HEAD), jnp.float32),
    )
    shards = lax.all_gather(key_vals, "blk", axis=0, tiled=True)
    shard_count = shards.shape[0] // tok_blk
    grouped = shards.reshape(shard_count, tok_blk, 2, width_here)

    def scan_step(state, element):
        number, segment = element
        return (absorb_one(state, segment, number * tok_blk), None)

    numbers = jnp.arange(shard_count, dtype=jnp.int32)
    result, unused = lax.scan(scan_step, start_state, (numbers, grouped))
    peak, totals, accum = result
    joint = accum / totals[:, :, None]
    partial_value = jnp.einsum(
        "jf,sfd->sjd", resample_mix, id_feats, preferred_element_type=jnp.float32
    )
    partial_rows = partial_value.reshape(SUBJ * IDTOK, width)
    pooled = lax.psum(partial_rows, "blk")
    latent_rows = jnp.tile(latents.astype(jnp.float32), (SUBJ, 1))
    id_tokens = normalize(latent_rows + pooled, id_gain)
    id_kv = jnp.einsum(
        "nd,dce->nce", id_tokens, id_kv_weight, preferred_element_type=jnp.float32
    ).astype(jnp.bfloat16)
    id_keys = id_kv[:, 0].reshape(SUBJ * IDTOK, heads_here, HEAD)
    id_values = id_kv[:, 1].reshape(SUBJ * IDTOK, heads_here, HEAD)
    block_pos = block_start + jnp.arange(tok_blk, dtype=jnp.int32)
    has_id = (region_ids > 0) & (block_pos >= TXT)
    subject = jnp.zeros((tok_blk,), jnp.int32)
    for which in range(SUBJ):
        subject = subject + jnp.where(region_ids == which + 1, region_identity[which], 0)
    key_subject = jnp.arange(SUBJ * IDTOK, dtype=jnp.int32) // IDTOK
    matches = (key_subject[None, :] == subject[:, None]) & has_id[:, None]
    id_scores = (
        jnp.einsum("qhe,nhe->qhn", queries, id_keys, preferred_element_type=jnp.float32)
        * score_scale
    )
    id_scores = jnp.where(matches[:, None, :], id_scores, -1e30)
    id_peak = jnp.max(id_scores, axis=-1, keepdims=True)
    id_expo = jnp.exp(id_scores - id_peak) * matches[:, None, :].astype(jnp.float32)
    id_totals = jnp.sum(id_expo, axis=-1) + jnp.where(has_id, 0.0, 1.0)[:, None]
    mixed = jnp.einsum(
        "qhn,nhe->qhe", id_expo.astype(jnp.bfloat16), id_values, preferred_element_type=jnp.float32
    )
    idpart = mixed / id_totals[:, :, None]
    mixed_heads = (joint + idpart).reshape(tok_blk, width_here).astype(jnp.bfloat16)
    summed = lax.psum_scatter(
        jnp.dot(mixed_heads, out_weight, preferred_element_type=jnp.float32),
        "uly",
        scatter_dimension=0,
        tiled=True,
    )
    return summed.astype(jnp.bfloat16)


def solution(mesh):
    placed = (
        P(("blk", "uly"), None, None),
        P(),
        P("blk"),
        P(),
        P(None, "blk", None),
        P(None, "blk"),
        P(),
        P(),
        P(None, None, "uly"),
        P("uly", None),
    )
    return jax.shard_map(
        on_device, mesh=mesh, in_specs=placed, out_specs=P(("blk", "uly"), None), check_vma=False
    )
```

profile of v0, /device:TPU:6, one launch (start us, length us, event | category | flops | bytes accessed | tf_op | source)
XLA Modules:
  0.0 846.3 jit_solution(17798004909733539533)
XLA Ops:
  6.5 2.6 fusion.37
  9.3 3.7 copy.41
  12.9 5.5 reshape.135
  18.4 24.2 %all_to_all.18 = bf16[8,2,36864]{2,1,0:T(2,128)(2,1)} all-to-all(bf16[8,2,36864]{2,1,0:T(2,128)(2,1)S(1)} %reshape.135), channel_id=1, replica_groups=mesh['blk'=32,'uly'=8] {'uly'}, dimensions={0} | all-to-all | bytes 2359296 | tf_op jit(solution)/shard_map/all_to_all | solution.py:39
  42.6 6.6 reshape.136
  49.2 4.2 copy.59
  57.7 3.3 select_add_fusion
  65.4 173.3 %all-reduce.2.cloned.1.call-done = f32[128,3072]{1,0:T(8,128)} async-done(((f32[128,3072]{1,0:T(8,128)}), f32[128,3072]{1,0:T(8,128)}) %all-reduce.2.cloned.1.call-update) | async-done | bytes 1572880 | tf_op jit(solution)/shard_map/psum | solution.py:88
  238.7 1.7 multiply_reduce_fusion
  242.1 3.2 fusion.32
  246.2 2.2 fusion.48
  249.7 132.2 %all-gather.2.cloned.1.call-done = bf16[16384,2,384]{2,0,1:T(8,128)(2,1)} async-done(((bf16[512,2,384]{2,0,1:T(8,128)(2,1)}), bf16[16384,2,384]{2,0,1:T(8,128)(2,1)}) %all-gather.2.cloned.1.call-update) | async-done | bytes 25165840 | tf_op jit(solution)/shard_map/all_gather | solution.py:72
  382.4 346.8 %while.15 = (s32[]{:T(128)}, f32[512,3]{0,1:T(4,128)S(1)}, f32[512,3]{0,1:T(4,128)S(1)}, f32[512,3,128]{0,2,1:T(8,128)}, s32[32]{0:T(128)}, /*index=5*/s32[1]{0:...) while((s32[]{:T(128)}, f32[512,3]{0,1:T(4,128)S(1)}, ...), condition=%wide.region_3.4_spmd.clone, body=%wide.region_0.3_spmd.clone.sunk | while | flops 411903488 | bytes 23302392 | solution.py:81
  385.4 2.1 constant_dynamic-slice_fusion.2
  396.2 2.1 constant_dynamic-slice_fusion.2
  407.1 2.1 constant_dynamic-slice_fusion.2
  417.9 2.1 constant_dynamic-slice_fusion.2
  428.8 2.1 constant_dynamic-slice_fusion.2
  439.6 2.1 constant_dynamic-slice_fusion.2
  450.4 2.1 constant_dynamic-slice_fusion.2
  461.3 2.1 constant_dynamic-slice_fusion.2
  472.1 2.1 constant_dynamic-slice_fusion.2
  482.9 2.1 constant_dynamic-slice_fusion.2
  493.8 2.1 constant_dynamic-slice_fusion.2
  504.6 2.1 constant_dynamic-slice_fusion.2
  515.5 2.1 constant_dynamic-slice_fusion.2
  526.3 2.1 constant_dynamic-slice_fusion.2
  537.1 2.1 constant_dynamic-slice_fusion.2
  548.0 2.1 constant_dynamic-slice_fusion.2
  558.8 2.1 constant_dynamic-slice_fusion.2
  569.6 2.1 constant_dynamic-slice_fusion.2
  580.5 2.1 constant_dynamic-slice_fusion.2
  591.3 2.1 constant_dynamic-slice_fusion.2
  602.2 2.1 constant_dynamic-slice_fusion.2
  613.0 2.1 constant_dynamic-slice_fusion.2
  623.8 2.1 constant_dynamic-slice_fusion.2
  634.7 2.1 constant_dynamic-slice_fusion.2
  645.5 2.1 constant_dynamic-slice_fusion.2
  656.4 2.1 constant_dynamic-slice_fusion.2
  667.2 2.1 constant_dynamic-slice_fusion.2
  678.0 2.1 constant_dynamic-slice_fusion.2
  688.9 2.1 constant_dynamic-slice_fusion.2
  699.7 2.1 constant_dynamic-slice_fusion.2
  710.5 2.1 constant_dynamic-slice_fusion.2
  721.4 2.1 constant_dynamic-slice_fusion.2
  730.8 4.5 fusion.49
  735.3 102.5 %reduce-scatter.2.cloned.1.call-done = f32[64,3072]{1,0:T(8,128)} async-done(((f32[512,3072]{1,0:T(8,128)}), f32[64,3072]{1,0:T(8,128)}) %reduce-scatter.2.cloned.1.call-update) | async-done | bytes 786448 | tf_op jit(solution)/shard_map/reduce_scatter | solution.py:116
  837.8 1.9 convert_element_type.39
  (544 shorter events, 271.5 us)
Async XLA Ops:
  6.5 724.3 %copy-start = (bf16[384,3072]{1,0:T(8,128)(2,1)S(1)}, bf16[384,3072]{1,0:T(8,128)(2,1)}, u32[]{:S(2)}) copy-start(bf16[384,3072]{1,0:T(8,128)(2,1)} %param.21) | copy-start | bytes 7077892
  6.5 2.7 copy-start.2
  6.5 232.2 %all-reduce.2.cloned.1.call-start = ((), (), s32[]{:S(2)}) async-start(), calls=%async_computation.3 | async-start | bytes 3145728 | tf_op jit(solution)/shard_map/psum | solution.py:88
  9.2 372.7 %all-gather.2.cloned.1.call-start = ((), (), s32[]{:S(2)}) async-start(), calls=%async_computation.2 | async-start | bytes 25952256 | tf_op jit(solution)/shard_map/all_gather | solution.py:72
  54.4 783.4 %reduce-scatter.2.cloned.1.call-start = ((), (), s32[]{:S(2)}) async-start(), calls=%async_computation.4 | async-start | bytes 7077888 | tf_op jit(solution)/shard_map/reduce_scatter | solution.py:116
  63.9 176.5 %copy-start.1 = (f32[32,3072]{1,0:T(8,128)S(1)}, f32[32,3072]{1,0:T(8,128)}, u32[]{:S(2)}) copy-start(f32[32,3072]{1,0:T(8,128)} %convert_element_type.32) | copy-start | bytes 1179652
  389.0 2.3 copy-start.4
  399.8 1.6 copy-start.3
  399.9 2.3 copy-start.4
  410.6 1.6 copy-start.3
  410.7 2.3 copy-start.4
  421.5 1.6 copy-start.3
  421.5 2.3 copy-start.4
  432.4 2.3 copy-start.4
  443.2 2.3 copy-start.4
  454.1 2.3 copy-start.4
  464.8 1.6 copy-start.3
  464.9 2.3 copy-start.4
  475.7 2.3 copy-start.4
  486.6 2.3 copy-start.4
  497.4 2.3 copy-start.4
  508.2 1.6 copy-start.3
  508.2 2.3 copy-start.4
  519.1 2.3 copy-start.4
  529.9 2.3 copy-start.4
  540.8 2.3 copy-start.4
  551.5 1.6 copy-start.3
  551.6 2.3 copy-start.4
  562.4 2.3 copy-start.4
  573.3 2.3 copy-start.4
  584.0 1.6 copy-start.3
  584.1 2.3 copy-start.4
  594.9 2.3 copy-start.4
  605.8 2.3 copy-start.4
  616.6 2.3 copy-start.4
  627.4 1.6 copy-start.3
  627.5 2.3 copy-start.4
  638.3 2.3 copy-start.4
  649.1 2.3 copy-start.4
  660.0 2.3 copy-start.4
  670.7 1.6 copy-start.3
  670.8 2.3 copy-start.4
  681.6 2.3 copy-start.4
  692.5 2.3 copy-start.4
  703.3 2.3 copy-start.4
  714.1 1.6 copy-start.3
  714.2 2.3 copy-start.4
  725.0 2.3 copy-start.4
  (54 other events, 63.9 us)
Sparse Core Ops, SparseCore 0:
  10.0 228.7 all-reduce.1
  240.7 141.2 all-gather.1
  735.4 102.3 reduce-scatter.1
where the time goes:
time: 853 us; the launch traced here: 846 us
  waiting for transfers between devices  408 us (48%)
  local copies, waits for them, and re-layouts  207 us (24%)
  matrix products  96.6 us (11%)
  other arithmetic  75.6 us (9%)
  blocking collectives  24.2 us (3%)
  loops' own time  21.4 us (3%)
  between operations  13.2 us (2%)
    psum x1, waiting for transfers between devices, on_device(): pooled = lax.psum(partial_rows, 'blk')  173 us
    dynamic_slice x96, local copies, waits for them, and re-layouts, on_device(): result, unused = lax.scan(scan_step, start_state, (numbers, grouped))  151 us
    all_gather x1, waiting for transfers between devices, on_device(): shards = lax.all_gather(key_vals, 'blk', axis=0, tiled=True)  132 us
    reduce_scatter x1, waiting for transfers between devices, on_device(): lax.psum_scatter(jnp.dot(mixed_heads, out_weight, preferred_element_type=...  103 us
    dot_general x32, matrix products, absorb_one(): jnp.einsum('qhe,khe->qhk', queries, keys_block, preferred_element_type=jn...  48.9 us
    or x32, other arithmetic, absorb_one(): usable = (positions >= TXT) | (positions < text_count[0])  38.3 us
    dot_general x32, matrix products, absorb_one(): jnp.einsum('qhk,khe->qhe', exponent.astype(jnp.bfloat16), values_block, p...  33.6 us
    while x224, local copies, waits for them, and re-layouts  27.8 us
  transfers between devices with their start and end apart: 3, of which 3 were waited for; matrix products, arithmetic and copies ran while one was open for 5% of the time, Pallas kernels for 0%

commit v1 on v0

v1 whole, which is shorter than its diff:
```python
import functools
import math

import jax
import jax.numpy as jnp
from jax import lax
from jax.experimental import pallas as pl
from jax.experimental.pallas import tpu as pltpu
from jax.sharding import Mesh
from jax.sharding import PartitionSpec as P

HEAD = 128
TXT = 512
SUBJ = 4
IDTOK = 32
SCALE2 = math.log2(math.e) / math.sqrt(HEAD)
LIMIT = 96.0
QT = 1024
SUB = 256
bf16 = jnp.bfloat16
f32 = jnp.float32
TRANSPOSED = (((1,), (1,)), ((), ()))
BLK = ("xl", "z", "c")
ULY = ("y", "xh")
SWAP = [(0, 1), (1, 0)]


def attn_kernel(count, first, last, *refs):
    refs = list(refs)
    usable = refs.pop(0)
    flag_in = None if first else refs.pop(0)
    q_ref = refs.pop(0)
    k_refs = [refs.pop(0) for _ in range(count)]
    v_refs = [refs.pop(0) for _ in range(count)]
    acc_in = None if first else refs.pop(0)
    if last:
        sums_ref, lr_ref, vx, longest, acc_ref = refs
    else:
        acc_ref, flag_ref, vx, longest = refs
    head = pl.program_id(0)
    tile = pl.program_id(1)
    keys = [r.shape[0] for r in k_refs]

    @pl.when(tile == 0)
    def _():
        best = jnp.float32(0)
        ones = jnp.ones((HEAD, HEAD), bf16)
        at = 0
        for i in range(count):
            k = k_refs[i][...].astype(f32)
            square = jnp.dot((k * k).astype(bf16), ones, preferred_element_type=f32)
            best = jnp.maximum(best, jnp.max(square))
            rows = lax.broadcasted_iota(jnp.int32, (keys[i], HEAD), 0)
            cols = lax.broadcasted_iota(jnp.int32, (keys[i], HEAD), 1)
            ok = rows < usable[i]
            vx[at : at + keys[i], 0:HEAD] = jnp.where(ok, v_refs[i][...].astype(f32), 0.0).astype(bf16)
            vx[at : at + keys[i], HEAD : 2 * HEAD] = jnp.where(ok & (cols < 64), 1.0, 0.0).astype(bf16)
            at += keys[i]
        longest[0] = best

    rows_here = q_ref.shape[0]
    q = q_ref[...].astype(f32) * SCALE2
    square = jnp.dot((q * q).astype(bf16), jnp.ones((HEAD, HEAD), bf16), preferred_element_type=f32)
    fast = jnp.max(square) * longest[0] * 1.05 <= LIMIT * LIMIT
    if not first:
        fast = fast & (flag_in[head, tile] == 0)
    if not last:
        flag_ref[head, tile] = jnp.where(fast, 0, 1)
    q_high = q.astype(bf16)
    q_low = (q - q_high.astype(f32)).astype(bf16)
    q_both = jnp.concatenate([q_high, q_low], axis=1)

    @pl.when(fast)
    def _():
        for start in range(0, rows_here, SUB):
            total = None if first else acc_in[start : start + SUB, :]
            at = 0
            for i in range(count):
                k = k_refs[i][...]
                kk = jnp.concatenate([k, k], axis=1)
                scores = lax.dot_general(
                    q_both[start : start + SUB], kk, TRANSPOSED, preferred_element_type=f32
                )
                p = jnp.exp2(scores).astype(bf16)
                part = jnp.dot(p, vx[at : at + keys[i], :], preferred_element_type=f32)
                total = part if total is None else total + part
                at += keys[i]
            acc_ref[start : start + SUB, :] = total

    @pl.when(jnp.logical_not(fast))
    def _():
        lane = lax.broadcasted_iota(jnp.int32, (rows_here, 2 * HEAD), 1)
        total = jnp.zeros((rows_here, 2 * HEAD), f32) if first else acc_in[...]
        at = 0
        for i in range(count):
            k = k_refs[i][...]
            kk = jnp.concatenate([k, k], axis=1)
            scores = lax.dot_general(q_both, kk, TRANSPOSED, preferred_element_type=f32)
            scores = jnp.where(lax.broadcasted_iota(jnp.int32, scores.shape, 1) < usable[i], scores, -1e30)
            peak = jnp.max(scores, axis=1, keepdims=True)
            old = jnp.where(total[:, HEAD : HEAD + 1] > 0, total[:, 2 * HEAD - 1 : 2 * HEAD], -1e30)
            new = jnp.maximum(old, peak)
            p = jnp.exp2(scores - new).astype(bf16)
            part = jnp.dot(p, vx[at : at + keys[i], :], preferred_element_type=f32)
            total = jnp.where(lane < 192, total * jnp.exp2(old - new) + part, new)
            at += keys[i]
        acc_ref[...] = total

    if last:
        sums_ref[...] = acc_ref[:, 0:HEAD].astype(bf16)
        turned = acc_ref[:, HEAD : 2 * HEAD].T
        lr_ref[0:1, :] = turned[0:1, :]
        lr_ref[1:2, :] = turned[HEAD - 1 : HEAD, :]


def attend(usable, flag, q, shards, acc, last=False):
    count, first = len(shards), acc is None
    rows = q.shape[0]
    tiles = rows // QT
    heads = q.shape[1] // HEAD
    smem = pl.BlockSpec(memory_space=pltpu.SMEM)
    acc_block = pl.BlockSpec((None, QT, 2 * HEAD), lambda h, t: (h, t, 0))
    in_specs, args = [smem], [usable]
    if not first:
        in_specs.append(smem)
        args.append(flag)
    in_specs.append(pl.BlockSpec((QT, HEAD), lambda h, t: (t, h)))
    args.append(q)
    for shift in (0, heads):
        for kv in shards:
            in_specs.append(pl.BlockSpec((kv.shape[0], HEAD), lambda h, t, s=shift: (0, s + h)))
            args.append(kv)
    if not first:
        in_specs.append(acc_block)
        args.append(acc)
    total = sum(kv.shape[0] for kv in shards)
    scratch = [pltpu.VMEM((total, 2 * HEAD), bf16), pltpu.SMEM((1,), f32)]
    if last:
        out_specs = [
            pl.BlockSpec((QT, HEAD), lambda h, t: (t, h)),
            pl.BlockSpec((None, 2, QT), lambda h, t: (h, 0, t)),
        ]
        out_shape = [
            jax.ShapeDtypeStruct((rows, heads * HEAD), bf16),
            jax.ShapeDtypeStruct((heads, 2, rows), f32),
        ]
        scratch.append(pltpu.VMEM((QT, 2 * HEAD), f32))
    else:
        out_specs = [acc_block, smem]
        out_shape = [
            jax.ShapeDtypeStruct((heads, rows, 2 * HEAD), f32),
            jax.ShapeDtypeStruct((heads, tiles), jnp.int32),
        ]
    return pl.pallas_call(
        functools.partial(attn_kernel, count, first, last),
        grid=(heads, tiles),
        in_specs=in_specs,
        out_specs=out_specs,
        out_shape=out_shape,
        scratch_shapes=scratch,
        cost_estimate=pl.CostEstimate(
            flops=heads * rows * total * 2048,
            bytes_accessed=12 * 2**20,
            transcendentals=heads * rows * total,
        ),
        compiler_params=pltpu.CompilerParams(vmem_limit_bytes=40 * 2**20),
    )(*args)


def id_kernel(q_ref, kv_ref, match_ref, out_ref):
    width = q_ref.shape[1]
    match = match_ref[...]
    lacking = 1.0 - jnp.max(match, axis=1, keepdims=True)
    for h in range(width // HEAD):
        cols = slice(h * HEAD, (h + 1) * HEAD)
        scores = lax.dot_general(
            q_ref[:, cols], kv_ref[:, cols], TRANSPOSED, preferred_element_type=f32
        ) * (1.0 / math.sqrt(HEAD))
        scores = jnp.where(match > 0, scores, -1e30)
        peak = jnp.max(scores, axis=1, keepdims=True)
        expo = jnp.exp(scores - peak) * match
        totals = jnp.sum(expo, axis=1, keepdims=True) + lacking
        v = kv_ref[:, width + h * HEAD : width + (h + 1) * HEAD]
        out_ref[:, cols] = jnp.dot(expo.astype(bf16), v, preferred_element_type=f32) / totals


def id_attend(q, id_kv, match):
    return pl.pallas_call(
        id_kernel,
        out_shape=jax.ShapeDtypeStruct(q.shape, f32),
        compiler_params=pltpu.CompilerParams(vmem_limit_bytes=32 * 2**20),
    )(q, id_kv, match)


def combine_kernel(place, keep, recv, lr_own, lr_core, lr_x, lr_far, id_ref, out_ref):
    slot = pl.program_id(0)
    rows = keep.shape[0]
    refs = [r[1:2, :] for r in (lr_own, lr_core, lr_x, lr_far)]
    sums = [r[0:1, :] for r in (lr_own, lr_core, lr_x, lr_far)]
    top = functools.reduce(jnp.maximum, refs)
    weight = [jnp.exp2(r - top) for r in refs]
    total = sum(w * s for w, s in zip(weight, sums))

    def column(row):
        return jnp.broadcast_to(row, (HEAD, rows)).T

    value = keep[...].astype(f32) * column(weight[0] / total)
    value = value + recv[...].astype(f32) * column(weight[1] / total)

    @pl.when(slot == 0)
    def _():
        out_ref[...] = (value + id_ref[...]).astype(bf16)

    @pl.when(slot == 1)
    def _():
        out_ref[...] = value.astype(bf16)


def combine(place, sums, recv, lr, lr_core, lr_x, lr_far, idpart):
    tokens, width = idpart.shape
    heads = width // HEAD
    data = pl.BlockSpec((tokens, HEAD), lambda s, h, p: (s, h))
    near = pl.BlockSpec((None, 2, tokens), lambda s, h, p: (h, 0, s))
    cross = pl.BlockSpec((None, 2, tokens), lambda s, h, p: (h, 0, 1 - s))
    return pl.pallas_call(
        combine_kernel,
        grid_spec=pltpu.PrefetchScalarGridSpec(
            num_scalar_prefetch=1,
            grid=(2, heads),
            in_specs=[
                data,
                data,
                near,
                near,
                cross,
                cross,
                pl.BlockSpec((tokens, HEAD), lambda s, h, p: (0, h)),
            ],
            out_specs=pl.BlockSpec((None, tokens, HEAD), lambda s, h, p: ((p[0] + s) % 2, 0, h)),
        ),
        out_shape=jax.ShapeDtypeStruct((2, tokens, width), bf16),
        compiler_params=pltpu.CompilerParams(vmem_limit_bytes=32 * 2**20),
    )(place, sums, recv, lr, lr_core, lr_x, lr_far, idpart)


def normalize(summed, mean_square, id_gain):
    return (summed * lax.rsqrt(mean_square + 1e-06) * id_gain).astype(bf16)


def identity_kv(id_feats, resample_mix, latents, id_gain, id_kv_weight, number):
    width_here = id_kv_weight.shape[2]
    width = id_kv_weight.shape[0]
    here = id_feats.shape[1]
    groups = width // width_here
    feats = lax.dynamic_slice_in_dim(id_feats, number * width_here, width_here, 2)
    feats = feats.reshape(SUBJ * here, width_here)
    mix_row = jnp.pad(resample_mix.reshape(1, IDTOK * here), ((0, 15), (0, width_here - IDTOK * here)))
    packed = lax.all_gather(jnp.concatenate([feats, mix_row], axis=0), BLK, axis=0)
    shards = packed.shape[0]
    feats_all = packed[:, : SUBJ * here].reshape(shards, SUBJ, here, width_here)
    mix_all = packed[:, SUBJ * here, : IDTOK * here].reshape(shards, IDTOK, here)
    pooled = jnp.einsum("bjf,bsfd->sjd", mix_all, feats_all, preferred_element_type=f32)
    own = lax.dynamic_slice_in_dim(latents, number * width_here, width_here, 1).astype(f32)
    summed = (own[None] + pooled).reshape(SUBJ * IDTOK, width_here)
    summed = lax.all_gather(summed, ULY, axis=0)
    mean_square = jnp.sum(summed * summed, axis=(0, 2), keepdims=True) / width
    tokens = normalize(summed, mean_square, id_gain.reshape(groups, 1, width_here))
    tokens = tokens.transpose(1, 0, 2).reshape(SUBJ * IDTOK, width)
    keys = jnp.dot(tokens, id_kv_weight[:, 0], preferred_element_type=f32)
    values = jnp.dot(tokens, id_kv_weight[:, 1], preferred_element_type=f32)
    return jnp.concatenate([keys, values], axis=1).astype(bf16)


def on_device(
    joint_qkv,
    text_count,
    region_ids,
    region_identity,
    id_feats,
    resample_mix,
    latents,
    id_gain,
    id_kv_weight,
    out_weight,
):
    z_size = lax.axis_size("z")
    y_size = lax.axis_size("y")
    uly = y_size * lax.axis_size("xh")
    tok_dev = joint_qkv.shape[0]
    tok_blk = tok_dev * uly
    width = joint_qkv.shape[2]
    here = width // uly
    my_xl, my_z, my_c = lax.axis_index("xl"), lax.axis_index("z"), lax.axis_index("c")
    number = lax.axis_index(ULY)

    by_group = joint_qkv.reshape(tok_dev, 3, uly, here)
    kv_out = jnp.concatenate([by_group[:, 1], by_group[:, 2]], axis=-1).transpose(1, 0, 2)
    q_out = by_group[:, 0].transpose(1, 0, 2)
    kv = lax.all_to_all(kv_out, ULY, 0, 0, tiled=True).reshape(tok_blk, 2 * here)
    q_own = lax.all_to_all(q_out, ULY, 0, 0, tiled=True).reshape(tok_blk, here)
    q_x = lax.ppermute(q_own, "xl", SWAP)
    q_pair = jnp.concatenate([q_own, q_x], axis=0)
    queries = jnp.concatenate([q_pair, lax.ppermute(q_pair, "c", SWAP)], axis=0)

    def limits(origin, halves):
        text_here = (my_xl == 0) & (my_c == 0) & (origin % z_size == 0)
        used = jnp.where(text_here, text_count[0], tok_blk)
        if not halves:
            return [used]
        half = tok_blk // 2
        return [jnp.minimum(used, half), jnp.clip(used - half, 0, half)]

    right = [(i, (i + 1) % z_size) for i in range(z_size)]
    left = [(i, (i - 1) % z_size) for i in range(z_size)]
    up, down = kv, kv
    steps = []
    held, marks = [kv], limits(my_z, False)
    for step in range(1, z_size // 2):
        up = lax.ppermute(up, "z", right)
        down = lax.ppermute(down, "z", left)
        held += [up, down]
        marks += limits(my_z - step + z_size, False) + limits(my_z + step, False)
        steps.append((held, marks))
        held, marks = [], []
    half = tok_blk // 2
    steps.append(
        (
            [lax.ppermute(up[:half], "z", right), lax.ppermute(down[half:], "z", left)],
            limits(my_z + z_size // 2, True),
        )
    )
    acc, flag = None, None
    for at, (held, marks) in enumerate(steps):
        usable = jnp.stack(marks).astype(jnp.int32)
        acc, flag = attend(usable, flag, queries, held, acc, last=at == len(steps) - 1)
    sums, lr = acc, flag

    id_kv = identity_kv(id_feats, resample_mix, latents, id_gain, id_kv_weight, number)
    block = (my_xl * z_size + my_z) * 2 + my_c
    position = block * tok_blk + jnp.arange(tok_blk, dtype=jnp.int32)
    has_id = (region_ids > 0) & (position >= TXT)
    subject = jnp.zeros((tok_blk,), jnp.int32)
    for which in range(SUBJ):
        subject = subject + jnp.where(region_ids == which + 1, region_identity[which], 0)
    key_subject = jnp.arange(SUBJ * IDTOK, dtype=jnp.int32) // IDTOK
    match = ((key_subject[None, :] == subject[:, None]) & has_id[:, None]).astype(f32)
    idpart = id_attend(q_own, id_kv, match)

    pair = 2 * tok_blk
    recv = lax.ppermute(sums[pair:], "c", SWAP)
    lr_near, lr_send = lr[:, :, :pair], lr[:, :, pair:]
    lr_core = lax.ppermute(lr_send, "c", SWAP)
    lr_x = lax.ppermute(lr_near, "xl", SWAP)
    lr_far = lax.ppermute(lr_send, ("xl", "c"), [(i, 3 - i) for i in range(4)])
    mixed = combine(my_xl[None], sums, recv, lr, lr_core, lr_x, lr_far, idpart)

    quarter = tok_blk // y_size
    mixed = mixed.reshape(2 * y_size, quarter, here)
    mixed = lax.all_to_all(mixed, ("xl", "y"), 0, 0, tiled=True)
    mixed = mixed.reshape(2, y_size, quarter, here).astype(f32)
    mixed = (mixed[0] + mixed[1]).astype(bf16)
    mixed = mixed.transpose(1, 0, 2).reshape(quarter, y_size * here)

    weight = lax.all_gather(out_weight, "y", axis=0).reshape(y_size * here, width)
    product = jnp.dot(mixed, weight, preferred_element_type=f32)
    my_xh = lax.axis_index("xh")
    mine = lax.dynamic_slice_in_dim(product, my_xh * tok_dev, tok_dev, 0)
    other = lax.dynamic_slice_in_dim(product, (1 - my_xh) * tok_dev, tok_dev, 0)
    return (mine + lax.ppermute(other.astype(bf16), "xh", SWAP).astype(f32)).astype(bf16)


def solution(mesh):
    fine = Mesh(mesh.devices.reshape(2, 8, 2, 4, 2), BLK + ULY)
    placed = (
        P(BLK + ULY, None, None),
        P(),
        P(BLK),
        P(),
        P(None, BLK, None),
        P(None, BLK),
        P(),
        P(),
        P(None, None, ULY),
        P(ULY, None),
    )
    return jax.shard_map(
        on_device, mesh=fine, in_specs=placed, out_specs=P(BLK + ULY, None), check_vma=False
    )
```

time: 853 us -> 316 us (0.37)
  waiting for transfers between devices: 408 us -> 107 us
  local copies, waits for them, and re-layouts: 207 us -> 25.7 us
  Pallas kernels: 0 us -> 102 us
  matrix products: 96.6 us -> 12.2 us
  other arithmetic: 75.6 us -> 8.65 us
  starting transfers between devices: 0.09 us -> 38.9 us
  blocking collectives: 24.2 us -> 0 us
  loops' own time: 21.4 us -> 0 us
    psum x1 -> x0, waiting for transfers between devices: 173 us -> none  [on_device(): pooled = lax.psum(partial_rows, 'blk')]
    dynamic_slice x96 -> x0, local copies, waits for them, and re-layouts: 151 us -> none  [on_device(): result, unused = lax.scan(scan_step, start_state, (numbers, grouped))]
    reduce_scatter x1 -> x0, waiting for transfers between devices: 103 us -> none  [on_device(): lax.psum_scatter(jnp.dot(mixed_heads, out_weight, preferred_element_type=...]
    pallas_call x0 -> x6, Pallas kernels: none -> 102 us  [the longest x4 98 us: attend(): pl.pallas_call(functools.partial(attn_kernel, count, first, last), grid=(...]
    dot_general x68 -> x4, matrix products: 94.4 us -> 12.2 us  [the longest x1 5.11 us: on_device(): product = jnp.dot(mixed, weight, preferred_element_type=f32)]
    all_gather x1 -> x3, waiting for transfers between devices: 132 us -> 66.6 us  [the longest x1 66.6 us: identity_kv(): lax.all_gather(jnp.concatenate([feats, mix_row], axis=0), BLK, axis=0)]
    or x32 -> x0, other arithmetic: 38.3 us -> none  [absorb_one(): usable = (positions >= TXT) | (positions < text_count[0])]
    while x224 -> x0, local copies, waits for them, and re-layouts: 27.8 us -> none
  transfers between devices with their start and end apart: 3 -> 21, of which waited for: 3 -> 6; matrix products, arithmetic and copies ran while one was open for 5% -> 10% of each run, Pallas kernels for 0% -> 33%
where the time goes in v1:
time: 316 us; the launch traced here: 309 us
  waiting for transfers between devices  107 us (34%)
  Pallas kernels  102 us (32%)
  starting transfers between devices  38.9 us (12%)
  local copies, waits for them, and re-layouts  25.7 us (8%)
  between operations  14.4 us (5%)
  matrix products  12.2 us (4%)
  other arithmetic  8.65 us (3%)
    pallas_call x4, Pallas kernels, attend(): pl.pallas_call(functools.partial(attn_kernel, count, first, last), grid=(...  98 us
    all_gather x1, waiting for transfers between devices, identity_kv(): lax.all_gather(jnp.concatenate([feats, mix_row], axis=0), BLK, axis=0)  66.6 us
    all_to_all x1, waiting for transfers between devices, on_device(): mixed = lax.all_to_all(mixed, ('xl', 'y'), 0, 0, tiled=True)  11.8 us
    ppermute x1, waiting for transfers between devices, on_device(): lax.ppermute(other.astype(bf16), 'xh', SWAP).astype(f32)  10.9 us
    slice x1, local copies, waits for them, and re-layouts, identity_kv(): keys = jnp.dot(tokens, id_kv_weight[:, 0], preferred_element_type=f32)  10.9 us
    ppermute x3, starting transfers between devices, on_device(): down = lax.ppermute(down, 'z', left)  9.12 us
    all_to_all x1, starting transfers between devices, on_device(): q_own = lax.all_to_all(q_out, ULY, 0, 0, tiled=True).reshape(tok_blk, here)  7.25 us
    unnamed x21, local copies, waits for them, and re-layouts  7.19 us
  transfers between devices with their start and end apart: 21, of which 6 were waited for; matrix products, arithmetic and copies ran while one was open for 10% of the time, Pallas kernels for 33%

profile of v1, /device:TPU:6, one launch (start us, length us, event | category | flops | bytes accessed | tf_op | source)
XLA Modules:
  0.0 309.4 jit_solution(16630528803997669772)
XLA Ops:
  6.5 0.8 copy.27
  7.5 0.6 fusion.11
  8.2 0.8 dynamic-slice_convert_fusion.1
  8.9 66.6 %all-gather.8.cloned.1.call-done = bf16[1536,384]{1,0:T(8,128)(2,1)} async-done(((bf16[48,384]{1,0:T(8,128)(2,1)}), bf16[1536,384]{1,0:T(8,128)(2,1)}) %all-gather.8.cloned.1.call-update) | async-done | bytes 1179664 | tf_op jit(solution)/shard_map/all_gather | solution.py:258
  75.5 1.2 slice.80
  76.8 0.9 slice.79
  77.7 0.3 copy.28
  78.1 1.1 fusion.2
  79.3 0.7 all-gather.10.cloned.1.call-update
  80.0 0.2 copy.40
  80.4 0.8 copy.56
  81.2 7.3 %all-to-all-start = ((bf16[8,64,384]{2,1,0:T(8,128)(2,1)}), bf16[8,64,384]{2,1,0:T(8,128)(2,1)S(1)}, u32[]{:S(2)}, u32[]{:S(2)}) async-start(bf16[8,64,384]{2,1,0:T(8,128)(2,1)} %bitcast.73), calls=%async_computation | async-start | bytes 786432 | tf_op jit(solution)/shard_map/all_to_all | solution.py:300
  89.3 1.0 maximum_bitcast_fusion
  90.3 0.7 fusion.16
  91.0 5.4 %all-to-all-done = bf16[8,64,384]{2,1,0:T(8,128)(2,1)S(1)} async-done(((bf16[8,64,384]{2,1,0:T(8,128)(2,1)}), bf16[8,64,384]{2,1,0:T(8,128)(2,1)S(1)}, u32[]{:S(2)}, u32[]{:S(2)}) %all-to-all-start) | async-done | bytes 393248 | tf_op jit(solution)/shard_map/all_to_all | solution.py:300
  96.3 6.2 %all-to-all-start.1 = ((bf16[8,64,768]{2,1,0:T(8,128)(2,1)}), bf16[8,64,768]{2,1,0:T(8,128)(2,1)S(1)}, u32[]{:S(2)}, u32[]{:S(2)}) async-start(bf16[8,64,768]{2,1,0:T(8,128)(2,1)} %maximum_bitcast_fusion), calls=%async_computation.1 | async-start | bytes 1572864 | tf_op jit(solution)/shard_map/all_to_all | solution.py:299
  102.6 2.4 select_add_fusion
  105.0 1.7 collective-permute-start
  107.0 6.7 %all-to-all-done.1 = bf16[8,64,768]{2,1,0:T(8,128)(2,1)S(1)} async-done(((bf16[8,64,768]{2,1,0:T(8,128)(2,1)}), bf16[8,64,768]{2,1,0:T(8,128)(2,1)S(1)}, u32[]{:S(2)}, u32[]{:S(2)}) %all-to-all-start.1) | async-done | bytes 786464 | tf_op jit(solution)/shard_map/all_to_all | solution.py:299
  113.7 1.2 collective-permute-start.2
  114.9 2.0 collective-permute-start.3
  117.0 5.2 %collective-permute-done = bf16[512,384]{1,0:T(8,128)(2,1)S(1)} collective-permute-done((bf16[512,384]{1,0:T(8,128)(2,1)S(1)}, bf16[512,384]{1,0:T(8,128)(2,1)S(1)}, u32[]{:S(2)}, u32[]{:S(2)}) %collective-permute-start) | collective-permute-done | bytes 393248 | tf_op jit(solution)/shard_map/ppermute | solution.py:301
  122.3 10.9 %fusion.13 = (bf16[3072,1,384]{2,1,0:T(2,128)(2,1)}, bf16[3072,1,384]{2,1,0:T(2,128)(2,1)}) fusion(bf16[3072,2,384]{2,1,0:T(2,128)(2,1)} %param.18), kind=kLoop, calls=%fused_computation.43 | loop fusion | bytes 9437184 | tf_op jit(solution)/shard_map/slice | solution.py:269
  133.3 3.7 %collective-permute-start.5 = (bf16[512,768]{1,0:T(8,128)(2,1)S(1)}, bf16[512,768]{1,0:T(8,128)(2,1)S(1)}, u32[]{:S(2)}, u32[]{:S(2)}) collective-permute-start(bf16[512,768]{1,0:T(8,128)(2,1)S(1)} %collective-permute-done.3.refs_4_.refs_7_), channel_id=1, source_target_pairs={{0,112},{16,0},{32,16},{48,32},{64,48},{80,64},{96,80},{112,96},{1... | collective-permute-start | bytes 2359304 | tf_op jit(solution)/shard_map/ppermute | solution.py:320
  137.2 29.5 %shard_map.100 = (f32[3,2048,256]{2,1,0:T(8,128)S(1)}, s32[3,2]{1,0:T(4,128)S(1)}) custom-call(s32[3]{0:T(128)S(1)} %pad_add_fusion.3.refs_0_, bf16[2048,384]{1,0:T(8,128)(2,1)S(1)} %pad_maximum_fusion.refs_1_.refs_2_, bf16[512,768]{1,0:T(8,128)(2,1)S(1)} %bitcast.88, bf16[512,768]{1,0:T(8,128)(2,1)S(1)} %collective-permute-done.2.refs_3_.refs_6_, ...), custom_call_target="tpu_custom_call" | custom-call | flops 19327352832 | bytes 12582912 | tf_op jit(solution)/shard_map/pallas_call | solution.py:154
  166.7 2.6 copy-done.3
  169.2 3.4 %collective-permute-start.7 = (bf16[512,768]{1,0:T(8,128)(2,1)S(1)}, bf16[512,768]{1,0:T(8,128)(2,1)S(1)}, u32[]{:S(2)}, u32[]{:S(2)}) collective-permute-start(bf16[512,768]{1,0:T(8,128)(2,1)S(1)} %collective-permute-done.5.refs_4_.refs_6_), channel_id=1, source_target_pairs={{0,112},{16,0},{32,16},{48,32},{64,48},{80,64},{96,80},{112,96},{1... | collective-permute-start | bytes 2359304 | tf_op jit(solution)/shard_map/ppermute | solution.py:320
  172.6 24.4 %shard_map.101 = (f32[3,2048,256]{2,1,0:T(8,128)S(1)}, s32[3,2]{1,0:T(4,128)S(1)}) custom-call(s32[2]{0:T(128)S(1)} %pad_add_fusion.2.refs_0_, s32[3,2]{1,0:T(4,128)S(1)} %get-tuple-element.13.refs_1_, bf16[2048,384]{1,0:T(8,128)(2,1)S(1)} %pad_maximum_fusion.refs_1_.refs_2_, bf16[512,768]{1,0:T(8,128)(2,1)S(1)} %collective-permute-done.4.refs_3_.refs_5_, ...), custom_call_target="tpu_custom_call" | custom-call | flops 12884901888 | bytes 12582912 | tf_op jit(solution)/shard_map/pallas_call | solution.py:154
  197.0 2.6 copy-done.2
  199.8 3.5 %collective-permute-start.9 = (bf16[256,768]{1,0:T(8,128)(2,1)S(1)}, bf16[256,768]{1,0:T(8,128)(2,1)S(1)}, u32[]{:S(2)}, u32[]{:S(2)}) collective-permute-start(bf16[256,768]{1,0:T(8,128)(2,1)S(1)} %slice.78), channel_id=1, source_target_pairs={{0,112},{16,0},{32,16},{48,32},{64,48},{80,64},{96,80},{112,96},{1... | collective-permute-start | bytes 1179656 | tf_op jit(solution)/shard_map/ppermute | solution.py:328
  203.3 24.4 %shard_map.102 = (f32[3,2048,256]{2,1,0:T(8,128)S(1)}, s32[3,2]{1,0:T(4,128)S(1)}) custom-call(s32[2]{0:T(128)S(1)} %pad_add_fusion.1.refs_0_, s32[3,2]{1,0:T(4,128)S(1)} %get-tuple-element.15.refs_1_, bf16[2048,384]{1,0:T(8,128)(2,1)S(1)} %pad_maximum_fusion.refs_1_.refs_2_, bf16[512,768]{1,0:T(8,128)(2,1)S(1)} %collective-permute-done.6.refs_3_.refs_5_, ...), custom_call_target="tpu_custom_call" | custom-call | flops 12884901888 | bytes 12582912 | tf_op jit(solution)/shard_map/pallas_call | solution.py:154
  227.7 19.8 %shard_map.103 = (bf16[2048,384]{1,0:T(8,128)(2,1)S(1)}, f32[3,2,2048]{2,1,0:T(2,128)S(1)}) custom-call(s32[2]{0:T(128)S(1)} %pad_add_fusion.refs_0_, s32[3,2]{1,0:T(4,128)S(1)} %get-tuple-element.17.refs_1_, bf16[2048,384]{1,0:T(8,128)(2,1)S(1)} %pad_maximum_fusion.refs_1_.refs_2_, bf16[256,768]{1,0:T(8,128)(2,1)S(1)} %collective-permute-done.8.refs_3_.refs_5_, ...), custom_call_target="tpu_custom_call" | custom-call | flops 6442450944 | bytes 12582912 | tf_op jit(solution)/shard_map/pallas_call | solution.py:154
  247.6 0.4 collective-permute-start.13
  248.0 1.0 slice.61
  249.1 2.0 collective-permute-start.12
  251.0 3.0 copy.31
  254.1 1.7 multiply_reduce_fusion
  255.9 0.5 multiply_convert_fusion
  256.4 3.0 fusion.3
  259.4 3.0 fusion.4
  262.4 0.8 shard_map.104.id_ref
  263.3 3.4 %shard_map.105 = bf16[2,512,384]{2,1,0:T(8,128)(2,1)} custom-call(s32[1]{0:T(128)} %bitcast.place, bf16[2048,384]{1,0:T(8,128)(2,1)S(1)} %get-tuple-element.19.keep, bf16[1024,384]{1,0:T(8,128)(2,1)S(1)} %collective-permute-done.10.recv, f32[3,2,2048]{2,1,0:T(2,128)S(1)} %get-tuple-element.20.lr_own, f32[3,2,1024]{2,1,0:T(2,128)S(1)} %collective-permute-done.11.lr_core, ...), custom_call_target="tpu_custom_call" | custom-call | tf_op jit(solution)/shard_map/pallas_call | solution.py:225
  266.7 5.7 %all-to-all-start.2 = ((bf16[8,128,384]{2,1,0:T(8,128)(2,1)}), bf16[8,128,384]{2,1,0:T(8,128)(2,1)S(1)}, u32[]{:S(2)}, u32[]{:S(2)}) async-start(bf16[8,128,384]{2,1,0:T(8,128)(2,1)} %bitcast.36), calls=%async_computation.2 | async-start | bytes 1572864 | tf_op jit(solution)/shard_map/all_to_all | solution.py:359
  272.4 11.8 %all-to-all-done.2 = bf16[8,128,384]{2,1,0:T(8,128)(2,1)S(1)} async-done(((bf16[8,128,384]{2,1,0:T(8,128)(2,1)}), bf16[8,128,384]{2,1,0:T(8,128)(2,1)S(1)}, u32[]{:S(2)}, u32[]{:S(2)}) %all-to-all-start.2) | async-done | bytes 786464 | tf_op jit(solution)/shard_map/all_to_all | solution.py:359
  284.3 5.1 %convolution_bitcast_fusion = f32[128,3072]{1,0:T(8,128)S(1)} fusion(bf16[4,384,3072]{2,1,0:T(8,128)(2,1)} %bitcast.90, f32[8,128,384]{2,1,0:T(8,128)S(1)} %convert_element_type.33), kind=kOutput, calls=%fused_computation | convolution fusion | flops 1208352768 | bytes 12582912 | tf_op jit(solution)/shard_map/dot_general | solution.py:365
  289.5 1.4 collective-permute-start.14
  290.9 10.9 %collective-permute-done.14 = bf16[64,3072]{1,0:T(8,128)(2,1)S(1)} collective-permute-done((bf16[64,3072]{1,0:T(8,128)(2,1)S(1)}, bf16[64,3072]{1,0:T(8,128)(2,1)S(1)}, u32[]{:S(2)}, u32[]{:S(2)}) %collective-permute-start.14) | collective-permute-done | bytes 393248 | tf_op jit(solution)/shard_map/ppermute | solution.py:369
  301.8 0.8 add_convert_fusion
  (64 shorter events, 2.4 us)
Async XLA Ops:
  6.5 0.9 copy-start
  6.5 69.0 %all-gather.8.cloned.1.call-start = ((), (), s32[]{:S(2)}) async-start(), calls=%async_computation.4 | async-start | bytes 1216512 | tf_op jit(solution)/shard_map/all_gather | solution.py:258
  8.1 242.9 %all-gather.6.cloned.1.call-start = ((), (), s32[]{:S(2)}) async-start(), calls=%async_computation.3 | async-start | bytes 1769472 | tf_op jit(solution)/shard_map/all_gather | solution.py:265
  78.1 1.9 copy-start.5
  79.3 205.0 %all-gather.10.cloned.1.call-start = ((), (), s32[]{:S(2)}) async-start(), calls=%async_computation.5 | async-start | bytes 11796480 | tf_op jit(solution)/shard_map/all_gather | solution.py:364
  81.2 15.2 %all-to-all-start = ((bf16[8,64,384]{2,1,0:T(8,128)(2,1)}), bf16[8,64,384]{2,1,0:T(8,128)(2,1)S(1)}, u32[]{:S(2)}, u32[]{:S(2)}) async-start(bf16[8,64,384]{2,1,0:T(8,128)(2,1)} %bitcast.73), calls=%async_computation | async-start | bytes 786432 | tf_op jit(solution)/shard_map/all_to_all | solution.py:300
  89.1 1.2 copy-start.8
  89.1 1.9 copy-start.7
  89.2 17.5 %copy-start.6 = (f32[3072]{0:T(1024)S(1)}, f32[3072]{0:T(1024)}, u32[]{:S(2)}) copy-start(f32[3072]{0:T(1024)} %param.17) | copy-start | bytes 36868
  96.3 17.4 %all-to-all-start.1 = ((bf16[8,64,768]{2,1,0:T(8,128)(2,1)}), bf16[8,64,768]{2,1,0:T(8,128)(2,1)S(1)}, u32[]{:S(2)}, u32[]{:S(2)}) async-start(bf16[8,64,768]{2,1,0:T(8,128)(2,1)} %maximum_bitcast_fusion), calls=%async_computation.1 | async-start | bytes 1572864 | tf_op jit(solution)/shard_map/all_to_all | solution.py:299
  105.0 17.1 %collective-permute-start = (bf16[512,384]{1,0:T(8,128)(2,1)S(1)}, bf16[512,384]{1,0:T(8,128)(2,1)S(1)}, u32[]{:S(2)}, u32[]{:S(2)}) collective-permute-start(bf16[512,384]{1,0:T(8,128)(2,1)S(1)} %bitcast.82), channel_id=1, source_target_pairs={{0,128},{128,0},{1,129},{129,1},{2,130},{130,2},{3,131},{131,3},{4... | collective-permute-start | bytes 1179656 | tf_op jit(solution)/shard_map/ppermute | solution.py:301
  113.7 19.4 %collective-permute-start.2 = (bf16[512,768]{1,0:T(8,128)(2,1)S(1)}, bf16[512,768]{1,0:T(8,128)(2,1)S(1)}, u32[]{:S(2)}, u32[]{:S(2)}) collective-permute-start(bf16[512,768]{1,0:T(8,128)(2,1)S(1)} %bitcast.86), channel_id=1, source_target_pairs={{0,16},{16,32},{32,48},{48,64},{64,80},{80,96},{96,112},{112,0},{1... | collective-permute-start | bytes 2359304 | tf_op jit(solution)/shard_map/ppermute | solution.py:319
  114.9 18.3 %collective-permute-start.3 = (bf16[512,768]{1,0:T(8,128)(2,1)S(1)}, bf16[512,768]{1,0:T(8,128)(2,1)S(1)}, u32[]{:S(2)}, u32[]{:S(2)}) collective-permute-start(bf16[512,768]{1,0:T(8,128)(2,1)S(1)} %bitcast.87), channel_id=1, source_target_pairs={{0,112},{16,0},{32,16},{48,32},{64,48},{80,64},{96,80},{112,96},{1... | collective-permute-start | bytes 2359304 | tf_op jit(solution)/shard_map/ppermute | solution.py:320
  122.2 14.8 %collective-permute-start.1 = (bf16[1024,384]{1,0:T(8,128)(2,1)S(1)}, bf16[1024,384]{1,0:T(8,128)(2,1)S(1)}, u32[]{:S(2)}, u32[]{:S(2)}) collective-permute-start(bf16[1024,384]{1,0:T(8,128)(2,1)S(1)} %pad_maximum_fusion.1), channel_id=1, source_target_pairs={{0,8},{8,0},{1,9},{9,1},{2,10},{10,2},{3,11},{11,3},{4,12},{12,4},... | collective-permute-start | bytes 2359304 | tf_op jit(solution)/shard_map/ppermute | solution.py:303
  133.2 36.1 %collective-permute-start.4 = (bf16[512,768]{1,0:T(8,128)(2,1)S(1)}, bf16[512,768]{1,0:T(8,128)(2,1)S(1)}, u32[]{:S(2)}, u32[]{:S(2)}) collective-permute-start(bf16[512,768]{1,0:T(8,128)(2,1)S(1)} %collective-permute-done.2.refs_3_.refs_6_), channel_id=1, source_target_pairs={{0,16},{16,32},{32,48},{48,64},{64,80},{80,96},{96,112},{112,0},{1... | collective-permute-start | bytes 2359304 | tf_op jit(solution)/shard_map/ppermute | solution.py:319
  133.3 36.0 %collective-permute-start.5 = (bf16[512,768]{1,0:T(8,128)(2,1)S(1)}, bf16[512,768]{1,0:T(8,128)(2,1)S(1)}, u32[]{:S(2)}, u32[]{:S(2)}) collective-permute-start(bf16[512,768]{1,0:T(8,128)(2,1)S(1)} %collective-permute-done.3.refs_4_.refs_7_), channel_id=1, source_target_pairs={{0,112},{16,0},{32,16},{48,32},{64,48},{80,64},{96,80},{112,96},{1... | collective-permute-start | bytes 2359304 | tf_op jit(solution)/shard_map/ppermute | solution.py:320
  166.6 2.6 copy-start.3
  169.2 30.4 %collective-permute-start.6 = (bf16[512,768]{1,0:T(8,128)(2,1)S(1)}, bf16[512,768]{1,0:T(8,128)(2,1)S(1)}, u32[]{:S(2)}, u32[]{:S(2)}) collective-permute-start(bf16[512,768]{1,0:T(8,128)(2,1)S(1)} %collective-permute-done.4.refs_3_.refs_5_), channel_id=1, source_target_pairs={{0,16},{16,32},{32,48},{48,64},{64,80},{80,96},{96,112},{112,0},{1... | collective-permute-start | bytes 2359304 | tf_op jit(solution)/shard_map/ppermute | solution.py:319
  169.2 30.5 %collective-permute-start.7 = (bf16[512,768]{1,0:T(8,128)(2,1)S(1)}, bf16[512,768]{1,0:T(8,128)(2,1)S(1)}, u32[]{:S(2)}, u32[]{:S(2)}) collective-permute-start(bf16[512,768]{1,0:T(8,128)(2,1)S(1)} %collective-permute-done.5.refs_4_.refs_6_), channel_id=1, source_target_pairs={{0,112},{16,0},{32,16},{48,32},{64,48},{80,64},{96,80},{112,96},{1... | collective-permute-start | bytes 2359304 | tf_op jit(solution)/shard_map/ppermute | solution.py:320
  197.0 2.6 copy-start.2
  199.6 28.0 %collective-permute-start.8 = (bf16[256,768]{1,0:T(8,128)(2,1)S(1)}, bf16[256,768]{1,0:T(8,128)(2,1)S(1)}, u32[]{:S(2)}, u32[]{:S(2)}) collective-permute-start(bf16[256,768]{1,0:T(8,128)(2,1)S(1)} %slice.77), channel_id=1, source_target_pairs={{0,16},{16,32},{32,48},{48,64},{64,80},{80,96},{96,112},{112,0},{1... | collective-permute-start | bytes 1179656 | tf_op jit(solution)/shard_map/ppermute | solution.py:328
  199.8 27.9 %collective-permute-start.9 = (bf16[256,768]{1,0:T(8,128)(2,1)S(1)}, bf16[256,768]{1,0:T(8,128)(2,1)S(1)}, u32[]{:S(2)}, u32[]{:S(2)}) collective-permute-start(bf16[256,768]{1,0:T(8,128)(2,1)S(1)} %slice.78), channel_id=1, source_target_pairs={{0,112},{16,0},{32,16},{48,32},{64,48},{80,64},{96,80},{112,96},{1... | collective-permute-start | bytes 1179656 | tf_op jit(solution)/shard_map/ppermute | solution.py:328
  247.5 15.7 %collective-permute-start.11 = (f32[3,2,1024]{2,1,0:T(2,128)S(1)}, f32[3,2,1024]{2,1,0:T(2,128)S(1)}, u32[]{:S(2)}, u32[]{:S(2)}) collective-permute-start(f32[3,2,1024]{2,1,0:T(2,128)S(1)} %get-tuple-element.27), channel_id=1, source_target_pairs={{0,8},{8,0},{1,9},{9,1},{2,10},{10,2},{3,11},{11,3},{4,12},{12,4},... | collective-permute-start | bytes 73736 | tf_op jit(solution)/shard_map/ppermute | solution.py:352
  247.6 15.6 %collective-permute-start.13 = (f32[3,2,1024]{2,1,0:T(2,128)S(1)}, f32[3,2,1024]{2,1,0:T(2,128)S(1)}, u32[]{:S(2)}, u32[]{:S(2)}) collective-permute-start(f32[3,2,1024]{2,1,0:T(2,128)S(1)} %get-tuple-element.27), channel_id=1, source_target_pairs={{0,136},{8,128},{128,8},{136,0},{1,137},{9,129},{129,9},{137,1},{2... | collective-permute-start | bytes 73736 | tf_op jit(solution)/shard_map/ppermute | solution.py:354
  248.9 14.3 %collective-permute-start.10 = (bf16[1024,384]{1,0:T(8,128)(2,1)}, bf16[1024,384]{1,0:T(8,128)(2,1)S(1)}, u32[]{:S(2)}, u32[]{:S(2)}) collective-permute-start(bf16[1024,384]{1,0:T(8,128)(2,1)} %slice.61), channel_id=1, source_target_pairs={{0,8},{8,0},{1,9},{9,1},{2,10},{10,2},{3,11},{11,3},{4,12},{12,4},... | collective-permute-start | bytes 2359304 | tf_op jit(solution)/shard_map/ppermute | solution.py:350
  249.1 14.2 %collective-permute-start.12 = (f32[3,2,1024]{2,1,0:T(2,128)S(1)}, f32[3,2,1024]{2,1,0:T(2,128)S(1)}, u32[]{:S(2)}, u32[]{:S(2)}) collective-permute-start(f32[3,2,1024]{2,1,0:T(2,128)S(1)} %get-tuple-element.26), channel_id=1, source_target_pairs={{0,128},{128,0},{1,129},{129,1},{2,130},{130,2},{3,131},{131,3},{4... | collective-permute-start | bytes 73736 | tf_op jit(solution)/shard_map/ppermute | solution.py:353
  254.1 1.9 copy-start.4
  266.7 17.5 %all-to-all-start.2 = ((bf16[8,128,384]{2,1,0:T(8,128)(2,1)}), bf16[8,128,384]{2,1,0:T(8,128)(2,1)S(1)}, u32[]{:S(2)}, u32[]{:S(2)}) async-start(bf16[8,128,384]{2,1,0:T(8,128)(2,1)} %bitcast.36), calls=%async_computation.2 | async-start | bytes 1572864 | tf_op jit(solution)/shard_map/all_to_all | solution.py:359
  284.3 18.3 %copy-start.1 = (bf16[4,8,3072]{2,1,0:T(8,128)(2,1)S(1)}, bf16[4,8,3072]{2,1,0:T(8,128)(2,1)}, u32[]{:S(2)}) copy-start(bf16[4,8,3072]{2,1,0:T(8,128)(2,1)} %param.14) | copy-start | bytes 589828
  289.5 12.3 %collective-permute-start.14 = (bf16[64,3072]{1,0:T(8,128)(2,1)S(1)}, bf16[64,3072]{1,0:T(8,128)(2,1)S(1)}, u32[]{:S(2)}, u32[]{:S(2)}) collective-permute-start(bf16[64,3072]{1,0:T(8,128)(2,1)S(1)} %dynamic-slice_convert_fusion), channel_id=1, source_target_pairs={{0,1},{1,0},{2,3},{3,2},{4,5},{5,4},{6,7},{7,6},{8,9},{9,8},{10,11... | collective-permute-start | bytes 1179656 | tf_op jit(solution)/shard_map/ppermute | solution.py:369
Sparse Core Ops, SparseCore 0:
  9.2 66.2 all-gather.7
  79.4 55.4 all-gather.5
  136.7 94.9 all-gather.9
